TPU v7x, 256 devices: a whole 4x4x8 slice. The times are simulated.
256 devices in a mesh: half: 2 (over z_hi), point: 64 (over z_lo, y, x), row: 2 (over core).
Axes of the slice: x: 4, y: 4, z: 8 (z_hi: 2, z_lo: 4; z = z_hi * 4 + z_lo), core: 2. Of those that a mesh axis runs over, the one named last changes fastest.
Arguments:
- children: float32 [2, 2048, 128, 128], P('half', 'point', 'row'), may hold values from -0.0390625 to 0.0390625
- residual_series: float32 [2048, 8192], P('point', ('row', 'half')), may hold values from -0.0390625 to 0.0390625
Outputs:
- basis_values: float32 [2, 2048, 128, 128], P(None, 'point', ('row', 'half'))
- residual_values: float32 [2, 2048, 8192], P(None, 'point', ('row', 'half'))
All inputs are finite; a program needn't handle non-finite values.
Results may differ from a plain program's by a relative error of at most 0.0001.
Values sent between devices are 32-bit elements; how exact they have to be, the bound alone decides.
A program may use at most 128 MiB of HBM per device.

v0:
```python
import math

import jax
import jax.numpy as jnp
from jax import lax
from jax.sharding import PartitionSpec as P

BLOCK = 64
LENGTH = 524288


def rotation(phases):
    wrapped = jnp.bitwise_and(phases, LENGTH - 1)
    radians = wrapped.astype(jnp.float32) * (2.0 * math.pi / LENGTH)
    return (jnp.cos(radians), jnp.sin(radians))


def evaluate(series, groups, within):
    entries = series.shape[1]
    stride = LENGTH // (groups * within)
    group_ids = jnp.arange(groups, dtype=jnp.int32)
    inner_ids = jnp.arange(within, dtype=jnp.int32)
    base_step = group_ids * stride + 1
    outer_cos, outer_sin = rotation((group_ids * within)[None, :] * base_step[:, None])
    twist_cos, twist_sin = rotation(inner_ids[None, :] * base_step[:, None])
    inner_cos, inner_sin = rotation(inner_ids[:, None] * inner_ids[None, :] * (LENGTH // within))
    folded = series.reshape(groups, within * entries)
    outer_re = jnp.dot(
        outer_cos, folded, precision=lax.Precision.HIGHEST, preferred_element_type=jnp.float32
    ).reshape(groups, within, entries)
    outer_im = jnp.dot(
        outer_sin, folded, precision=lax.Precision.HIGHEST, preferred_element_type=jnp.float32
    ).reshape(groups, within, entries)
    turned_re = outer_re * twist_cos[:, :, None] - outer_im * twist_sin[:, :, None]
    turned_im = outer_re * twist_sin[:, :, None] + outer_im * twist_cos[:, :, None]
    hp = lax.Precision.HIGHEST
    value_re = jnp.einsum("st,qte->qse", inner_cos, turned_re, precision=hp) - jnp.einsum(
        "st,qte->qse", inner_sin, turned_im, precision=hp
    )
    value_im = jnp.einsum("st,qte->qse", inner_cos, turned_im, precision=hp) + jnp.einsum(
        "st,qte->qse", inner_sin, turned_re, precision=hp
    )
    return jnp.stack(
        [value_re.reshape(groups * within, entries), value_im.reshape(groups * within, entries)]
    )


def complex_product(left_factor, right_factor):
    hp = lax.Precision.HIGHEST
    real_part = jnp.einsum(
        "cik,ckj->cij", left_factor[0], right_factor[0], precision=hp
    ) - jnp.einsum("cik,ckj->cij", left_factor[1], right_factor[1], precision=hp)
    imag_part = jnp.einsum(
        "cik,ckj->cij", left_factor[0], right_factor[1], precision=hp
    ) + jnp.einsum("cik,ckj->cij", left_factor[1], right_factor[0], precision=hp)
    return jnp.stack([real_part, imag_part])


def spectrum(stacked, groups, within):
    by_entry = lax.all_to_all(stacked, "point", split_axis=1, concat_axis=0, tiled=True)
    return lax.all_to_all(
        evaluate(by_entry, groups, within), "point", split_axis=1, concat_axis=2, tiled=True
    )


def per_device(children, residual_series):
    within = residual_series.shape[0]
    groups = lax.axis_size("point")
    row_count = children.shape[2]
    col_count = children.shape[3]
    tile_size = row_count * col_count
    row_share = row_count // 2
    row_start = lax.axis_index("half") * row_share
    gathered = lax.all_gather(children, "half", axis=0, tiled=True)
    stacked = jnp.concatenate(
        [
            gathered[0].reshape(within, tile_size),
            gathered[1].reshape(within, tile_size),
            residual_series,
        ],
        axis=1,
    )
    spectra = spectrum(stacked, groups, within)
    lower_values = spectra[:, :, :tile_size].reshape(2, within, row_count, col_count)
    upper_values = spectra[:, :, tile_size : 2 * tile_size].reshape(2, within, row_count, col_count)
    series_values = spectra[:, :, 2 * tile_size :]
    series_rows = lax.all_gather(series_values, "half", axis=2, tiled=True)
    lower_all, series_all = (
        lax.all_gather(lower_values.reshape(2, within, tile_size), "row", axis=2, tiled=True),
        lax.all_gather(series_rows, "row", axis=2, tiled=True),
    )
    lower_full = lower_all.reshape(2, within, col_count, col_count)
    series_full = series_all.reshape(2, within, col_count, BLOCK)
    upper_part = lax.dynamic_slice_in_dim(upper_values, row_start, row_share, 2)
    lower_part = lax.dynamic_slice_in_dim(lower_values, row_start, row_share, 2)
    basis_values = complex_product(upper_part, lower_full)
    residual_values = complex_product(lower_part, series_full).reshape(2, within, row_share * BLOCK)
    return (basis_values, residual_values)


def solution(mesh):
    placed = (P("half", "point", "row", None), P("point", ("row", "half")))
    return jax.shard_map(
        per_device,
        mesh=mesh,
        in_specs=placed,
        out_specs=(P(None, "point", ("row", "half"), None), P(None, "point", ("row", "half"))),
        check_vma=False,
    )
```

profile of v0, /device:TPU:1, one launch (start us, length us, event | category | flops | bytes accessed | tf_op | source)
XLA Modules:
  0.0 516.3 jit_solution(10069010873291753464)
XLA Ops:
  7.2 0.7 all-gather.5.cloned.1.call-update
  7.9 70.9 %all-gather.5.cloned.1.call-done = f32[2,32,64,128]{3,2,1,0:T(8,128)} async-done(((f32[1,32,64,128]{3,2,1,0:T(8,128)}), f32[2,32,64,128]{3,2,1,0:T(8,128)}) %all-gather.5.cloned.1.call-update) | async-done | bytes 2097168 | tf_op jit(solution)/shard_map/all_gather | solution.py:74
  78.8 1.7 fusion.86
  80.5 1.2 copy_bitcast_fusion
  81.7 1.6 pad_maximum_fusion.1
  83.3 3.4 all_to_all.25
  86.7 3.4 copy.32
  90.2 7.4 %all-to-all-start = ((f32[32,64,288]{2,0,1:T(8,128)}), f32[32,64,288]{2,0,1:T(8,128)S(1)}, u32[]{:S(2)}, u32[]{:S(2)}) async-start(f32[32,64,288]{2,0,1:T(8,128)} %copy.32), calls=%async_computation | async-start | bytes 6291456 | tf_op jit(solution)/shard_map/all_to_all | solution.py:60
  97.8 71.3 %all-to-all-done = f32[32,64,288]{2,0,1:T(8,128)S(1)} async-done(((f32[32,64,288]{2,0,1:T(8,128)}), f32[32,64,288]{2,0,1:T(8,128)S(1)}, u32[]{:S(2)}, u32[]{:S(2)}) %all-to-all-start) | async-done | bytes 2359328 | tf_op jit(solution)/shard_map/all_to_all | solution.py:60
  169.1 2.7 reshape.88
  171.8 3.6 dot_general.47
  175.4 4.7 fusion.10
  180.1 5.3 %multiply_subtract_fusion = (f32[64,32,288]{2,0,1:T(8,128)S(1)}, f32[64,32,288]{2,0,1:T(8,128)S(1)}) fusion(f32[64,32,288]{2,0,1:T(8,128)S(1)} %fusion.10, f32[64,32]{0,1:T(8,128)S(1)} %get-tuple-element.13, f32[64,32]{0,1:T(8,128)S(1)} %get-tuple-element.12, f32[32,288,64]{1,0,2:T(8,128)S(1)} %dot_general.47, s32[64]{0:T(128)S(1)} %get-tuple-element.16, ...), kind=kOutput, calls=%fused_computation.2 | convolution fusion | flops 456540160 | bytes 9454080 | tf_op jit(solution)/shard_map/dot_general | solution.py:31
  185.4 5.3 %fusion.2 = f32[64,288,32]{1,2,0:T(8,128)S(1)} fusion(f32[64,32,288]{2,0,1:T(8,128)S(1)} %get-tuple-element.3), kind=kOutput, calls=%fused_computation.5 | convolution fusion | flops 226497536 | bytes 4718592 | tf_op jit(solution)/shard_map/st,qte->qse/dot_general | solution.py:37
  190.7 4.9 fusion
  195.6 4.9 fusion.12
  200.6 23.7 %copy.39 = f32[1,2048,288]{2,0,1:T(1,128)S(1)} copy(f32[1,2048,288]{2,1,0:T(8,128)S(1)} %bitcast.93) | data formatting | bytes 4718592 | tf_op jit(solution)/shard_map/stack;reshape | solution.py:43
  224.3 4.9 fusion.15
  229.3 23.6 %copy.40 = f32[1,2048,288]{2,0,1:T(1,128)S(1)} copy(f32[1,2048,288]{2,1,0:T(8,128)S(1)} %bitcast.92) | data formatting | bytes 4718592 | tf_op jit(solution)/shard_map/stack;reshape | solution.py:43
  252.9 7.1 %pad_maximum_fusion = f32[2,2048,288]{2,0,1:T(2,128)S(1)} fusion(f32[1,2048,288]{2,0,1:T(1,128)S(1)} %copy.40, f32[1,2048,288]{2,0,1:T(1,128)S(1)} %copy.39), kind=kLoop, calls=%fused_computation | loop fusion | flops 1179648 | bytes 9437184 | tf_op jit(solution)/shard_map/stack | solution.py:43
  260.0 145.3 %all_to_all.34 = f32[2,2048,288]{2,0,1:T(2,128)S(1)} all-to-all(f32[2,2048,288]{2,0,1:T(2,128)S(1)} %pad_maximum_fusion), channel_id=1, replica_groups=mesh['half'=2,'point'=64,'row'=2] {'point'}, dimensions={1} | all-to-all | bytes 9437184 | tf_op jit(solution)/shard_map/all_to_all | solution.py:61
  405.4 6.3 %copy.41 = f32[2,32,64,288]{3,2,1,0:T(8,128)} copy(f32[2,32,64,288]{3,0,1,2:T(2,128)S(1)} %bitcast.85) | data formatting | bytes 9437184 | tf_op jit(solution)/shard_map/all_to_all | solution.py:61
  411.6 6.9 %all_to_all.31 = f32[2,32,18432]{2,1,0:T(8,128)} reshape(f32[2,32,64,288]{3,2,1,0:T(8,128)} %copy.41) | data formatting | bytes 9437184 | tf_op jit(solution)/shard_map/all_to_all | solution.py:61
  418.6 1.9 slice.70
  420.5 38.3 %all-gather.9.cloned.1.call-done = f32[2,32,4096]{2,1,0:T(8,128)} async-done(((f32[2,32,2048]{2,1,0:T(8,128)}), f32[2,32,4096]{2,1,0:T(8,128)}) %all-gather.9.cloned.1.call-update) | async-done | bytes 1048592 | tf_op jit(solution)/shard_map/all_gather | solution.py:87
  458.9 4.6 fusion.84
  463.6 1.5 copy-done.1
  465.1 1.8 copy.55
  466.9 1.8 copy.52
  468.7 4.9 all-gather.11.cloned.1.call-done
  473.6 2.7 fusion.85
  476.3 2.2 squeeze.37
  478.5 2.2 squeeze.39
  480.7 3.1 fusion.23
  483.8 3.0 convolution_subtract_fusion
  487.0 4.0 fusion.22
  491.0 3.0 convolution_add_fusion
  494.1 0.8 pad_maximum_fusion.3
  495.0 0.6 all-gather.7.cloned.1.call-done
  495.6 2.5 slice_bitcast_fusion.1
  498.1 0.4 copy.53
  498.5 0.4 copy.54
  498.9 1.2 copy-done.2
  500.1 2.0 fusion.21
  502.1 2.2 fusion.20
  504.3 2.0 fusion.19
  506.3 2.0 fusion.18
  508.3 1.0 pad_maximum_fusion.2
  (19 shorter events, 0.7 us)
Async XLA Ops:
  7.2 71.6 %all-gather.5.cloned.1.call-start = ((), (), s32[]{:S(2)}) async-start(), calls=%async_computation.2 | async-start | bytes 3145728 | tf_op jit(solution)/shard_map/all_gather | solution.py:74
  80.5 1.2 copy-start.4
  90.2 78.9 %all-to-all-start = ((f32[32,64,288]{2,0,1:T(8,128)}), f32[32,64,288]{2,0,1:T(8,128)S(1)}, u32[]{:S(2)}, u32[]{:S(2)}) async-start(f32[32,64,288]{2,0,1:T(8,128)} %copy.32), calls=%async_computation | async-start | bytes 6291456 | tf_op jit(solution)/shard_map/all_to_all | solution.py:60
  97.6 361.2 %all-gather.9.cloned.1.call-start = ((), (), s32[]{:S(2)}) async-start(), calls=%async_computation.4 | async-start | bytes 1572864 | tf_op jit(solution)/shard_map/all_gather | solution.py:87
  420.4 53.2 %all-gather.11.cloned.1.call-start = ((), (), s32[]{:S(2)}) async-start(), calls=%async_computation.5 | async-start | bytes 3145728 | tf_op jit(solution)/shard_map/all_gather | solution.py:90
  458.9 36.7 %all-gather.7.cloned.1.call-start = ((), (), s32[]{:S(2)}) async-start(), calls=%async_computation.3 | async-start | bytes 6291456 | tf_op jit(solution)/shard_map/all_gather | solution.py:89
  463.6 1.6 copy-start.1
  463.6 3.3 copy-start.3
  480.7 3.1 copy-start
  498.5 1.6 copy-start.2
Sparse Core Ops, SparseCore 0:
  9.8 68.9 all-gather.4
  420.6 38.2 all-gather.8
  460.6 12.9 all-gather.10
  475.3 20.2 all-gather.6
where the time goes:
time: 523 us; the launch traced here: 516 us
  waiting for transfers between devices  187 us (36%)
  blocking collectives  145 us (28%)
  local copies, waits for them, and re-layouts  100 us (19%)
  matrix products  51.3 us (10%)
  between operations  14.4 us (3%)
  other arithmetic  10.7 us (2%)
  starting transfers between devices  7.59 us (1%)
    all_to_all x1, blocking collectives, spectrum(): lax.all_to_all(evaluate(by_entry, groups, within), 'point', split_axis=1,...  145 us
    all_to_all x1, waiting for transfers between devices, spectrum(): lax.all_to_all(stacked, 'point', split_axis=1, concat_axis=0, tiled=True)  71.3 us
    all_gather x1, waiting for transfers between devices, per_device(): gathered = lax.all_gather(children, 'half', axis=0, tiled=True)  70.9 us
    another operation x2, local copies, waits for them, and re-layouts, evaluate(): jnp.stack([value_re.reshape(groups * within, entries), value_im.reshape(g...  47.3 us
    all_gather x1, waiting for transfers between devices, per_device(): series_rows = lax.all_gather(series_values, 'half', axis=2, tiled=True)  38.3 us
    all_to_all x2, local copies, waits for them, and re-layouts, spectrum(): lax.all_to_all(evaluate(by_entry, groups, within), 'point', split_axis=1,...  13.2 us
  transfers between devices with their start and end apart: 5, of which 5 were waited for; matrix products, arithmetic and copies ran while one was open for 6% of the time, Pallas kernels for 0%

commit v1 on v0

v1 whole, which is shorter than its diff:
```python
import math

import jax
import jax.numpy as jnp
import numpy as np
from jax import lax
from jax.experimental import pallas as pl
from jax.experimental.pallas import tpu as pltpu
from jax.sharding import PartitionSpec as P

BASIS = 128
BLOCK = 64
LENGTH = 524288
WITHIN = 32
GROUPS = 64
PLANE = 16
RING = 8
WAVES = 5
HOPS = 5
PARTS = 4
SLAB = PLANE * WITHIN
PART = SLAB // PARTS
MESH = pl.DeviceIdType.MESH
F32 = jnp.float32
BF16 = jnp.bfloat16


def split_matrix(matrix):
    matrix = matrix.astype(np.float32)
    high = matrix.astype(jnp.bfloat16)
    low = (matrix - high.astype(np.float32)).astype(jnp.bfloat16)
    return np.concatenate([high, high, low, low], axis=-1)


def transform_matrices():
    q = np.arange(GROUPS).reshape(4, PLANE)
    p = np.arange(GROUPS)
    phase = (32 * p[None, None, :] * (256 * q[:, :, None] + 1)) % LENGTH
    angle = phase * (2.0 * math.pi / LENGTH)
    outer = np.concatenate([np.cos(angle), np.sin(angle)], axis=1)
    t = np.arange(WITHIN)
    s = np.arange(WITHIN)
    phase = t[None, None, None, :] * (s[None, None, :, None] * 16384 + 256 * q[:, :, None, None] + 1)
    angle = (phase % LENGTH) * (2.0 * math.pi / LENGTH)
    cos, sin = np.cos(angle), np.sin(angle)
    real = np.concatenate([cos, -sin], axis=-1).reshape(4, PLANE, 2, 1, 16, 64)
    imag = np.concatenate([sin, cos], axis=-1).reshape(4, PLANE, 2, 1, 16, 64)
    inner = np.concatenate([real, imag], axis=3).reshape(4, PLANE * 64, 64)
    return split_matrix(outer), split_matrix(inner)


def halves(x):
    high = x.astype(BF16)
    return high, (x - high.astype(F32)).astype(BF16)


def stacked_halves(x):
    high, low = halves(x)
    return jnp.concatenate([high, low, high, low], axis=0)


def dot(a, b):
    return jnp.dot(a, b, preferred_element_type=F32)


def rows(offset, count):
    return pl.ds(pl.multiple_of(offset, 8), count)


def reach(wave, source, direction):
    if wave == 4:
        return 4 if direction == 0 else 3
    lower = source + 2 if direction == 0 else 5 - source
    if wave % 2 == 1:
        upper = 7 - source if direction == 0 else source - 4
    elif direction == 0:
        upper = jnp.where(source >= 6, 11 - source, 0)
    else:
        upper = jnp.where(source <= 5, source, 0)
    return jnp.where(source < 4, lower, upper)


def kernel(
    child, series, outer_all, inner_all, basis_out, residual_out,
    gathered, sending, mid, spectra, received, products, pairs, mixed, lanes, outer, inner,
    a_send, a_recv, own_sem, z_send, z_recv, d_send, d_recv, const_sem, out_local, out_send, out_recv,
):
    half = lax.axis_index("half")
    point = lax.axis_index("point")
    core = lax.axis_index("row")
    z = point // 16
    plane = point % 16
    y = plane // 4
    x = plane % 4
    ring = half * 4 + z

    def plane_peer(i):
        dy, dx = (i // 4) % 4, i % 4
        return ((y + dy) % 4) * 4 + (x + dx) % 4

    def ring_device(position):
        return (position // 4, (position % 4) * 16 + plane, core)

    consts = [
        pltpu.make_async_copy(outer_all.at[z], outer, const_sem.at[0]),
        pltpu.make_async_copy(inner_all.at[z], inner, const_sem.at[1]),
    ]
    for copy in consts:
        copy.start()

    barrier = pltpu.get_barrier_semaphore()

    def greet(i, carry):
        peer = plane_peer(i)
        pl.semaphore_signal(barrier, inc=1, device_id=(half, z * 16 + peer, (core + i // 16) % 2), device_id_type=MESH)
        return carry

    lax.fori_loop(1, 32, greet, 0)
    for step in (1, 7):
        pl.semaphore_signal(barrier, inc=1, device_id=ring_device((ring + step) % 8), device_id_type=MESH)

    for wave in range(WAVES):
        for m in range(PLANE):
            base = (wave * PLANE + m) * WITHIN
            if wave < 4:
                row = (wave % 2) * 32 + 2 * m + wave // 2
                sending[pl.ds(base, WITHIN), :] = child[pl.ds(row, WITHIN, stride=64), :]
            else:
                sending[pl.ds(base, WITHIN), :] = series[:, m * 128 : (m + 1) * 128]
    pl.semaphore_wait(barrier, 33)

    def slab(source, wave):
        return (source * WAVES + wave) * SLAB

    for wave in range(WAVES):
        own = slab(ring, wave) + plane * WITHIN

        def spread(i, carry):
            peer = plane_peer(i)
            pltpu.make_async_remote_copy(
                src_ref=sending.at[rows((wave * PLANE + peer) * WITHIN, WITHIN)],
                dst_ref=gathered.at[rows(own, WITHIN)],
                send_sem=a_send.at[wave],
                recv_sem=a_recv.at[wave],
                device_id=(half, z * 16 + peer, core),
                device_id_type=MESH,
            ).start()
            return carry

        lax.fori_loop(1, PLANE, spread, 0)
        pltpu.make_async_copy(
            sending.at[rows((wave * PLANE + plane) * WITHIN, WITHIN)], gathered.at[rows(own, WITHIN)], own_sem.at[wave]
        ).start()

    def spread_wait(wave):
        own = slab(ring, wave)
        count = (PLANE - 1) * WITHIN
        pltpu.make_async_remote_copy(
            src_ref=sending.at[pl.ds(wave * SLAB, count)],
            dst_ref=gathered.at[rows(own, count)],
            send_sem=a_send.at[wave],
            recv_sem=a_recv.at[wave],
            device_id=(half, point, 1 - core),
            device_id_type=MESH,
        ).wait()
        pltpu.make_async_copy(
            sending.at[pl.ds(0, WITHIN)], gathered.at[rows(own, WITHIN)], own_sem.at[wave]
        ).wait()

    def ring_copy(wave, direction, hop, part, source):
        place = rows(slab(source, wave) + part * PART, PART)
        target = ring_device((ring + (1 if direction == 0 else 7)) % 8)
        index = ((wave * 2 + direction) * HOPS + hop) * PARTS + part
        return pltpu.make_async_remote_copy(
            src_ref=gathered.at[place],
            dst_ref=gathered.at[place],
            send_sem=z_send.at[index],
            recv_sem=z_recv.at[index],
            device_id=target,
            device_id_type=MESH,
        )

    def origin(direction, hop):
        return (ring + (8 - hop if direction == 0 else hop)) % 8

    def begin(wave):
        for part in range(PARTS):
            for direction in range(2):

                @pl.when(reach(wave, ring, direction) >= 1)
                def _():
                    ring_copy(wave, direction, 0, part, ring).start()

    def relay(wave, hop):
        for part in range(PARTS):
            for direction in range(2):
                source = origin(direction, hop)
                extent = reach(wave, source, direction)

                @pl.when(extent >= hop)
                def _():
                    ring_copy(wave, direction, hop - 1, part, source).wait_recv()
                    if hop < HOPS:

                        @pl.when(extent >= hop + 1)
                        def _():
                            ring_copy(wave, direction, hop, part, source).start()

    def ring_finish():
        for wave in range(WAVES):
            for hop in range(HOPS):
                for direction in range(2):
                    source = origin(direction, hop)

                    @pl.when(reach(wave, source, direction) >= hop + 1)
                    def _():
                        for part in range(PARTS):
                            ring_copy(wave, direction, hop, part, source).wait_send()

    def transform(first, wave, slot, place):
        def over_t(step, carry):
            columns = []
            for k in range(2):
                t = step * 2 + k
                column = jnp.concatenate(
                    [gathered[pl.ds(slab(first + i, wave) + t, PLANE, stride=WITHIN), :] for i in range(4)], axis=0
                )
                columns.append(stacked_halves(column))
            out = dot(outer[...], jnp.concatenate(columns, axis=1))
            for k in range(2):
                t = step * 2 + k
                mid[rows(t * PLANE, PLANE), :] = out[:PLANE, k * 128 : (k + 1) * 128]
                mid[rows((WITHIN + t) * PLANE, PLANE), :] = out[PLANE:, k * 128 : (k + 1) * 128]
            return carry

        lax.fori_loop(0, WITHIN // 2, over_t, 0, unroll=2)

        def over_q(q, carry):
            values = mid[pl.ds(q, 2 * WITHIN, stride=PLANE), :]
            out = dot(inner[rows(q * 64, 64), :], stacked_halves(values))
            spectra[rows(slot * 1024 + q * 64, 64), :] = out
            return carry

        lax.fori_loop(0, PLANE, over_q, 0, unroll=2)

        def back(i, carry):
            peer = plane_peer(i)
            other = (core + i // 16) % 2
            pltpu.make_async_remote_copy(
                src_ref=spectra.at[rows(slot * 1024 + peer * 64 + other * 32, 32)],
                dst_ref=received.at[rows(place * 32, 32)],
                send_sem=d_send.at[slot],
                recv_sem=d_recv.at[slot],
                device_id=(half, z * 16 + peer, other),
                device_id_type=MESH,
            ).start()
            return carry

        lax.fori_loop(1, 32, back, 0)
        pltpu.make_async_copy(
            spectra.at[rows(slot * 1024 + plane * 64 + core * 32, 32)], received.at[rows(place * 32, 32)], own_sem.at[WAVES + slot]
        ).start()

    def back_wait(slot):
        pltpu.make_async_remote_copy(
            src_ref=spectra.at[pl.ds(slot * 1024, 31 * 32)],
            dst_ref=received.at[pl.ds(0, 31 * 32)],
            send_sem=d_send.at[slot],
            recv_sem=d_recv.at[slot],
            device_id=(half, point, 1 - core),
            device_id_type=MESH,
        ).wait()
        pltpu.make_async_copy(
            spectra.at[pl.ds(0, 32)], received.at[pl.ds(0, 32)], own_sem.at[WAVES + slot]
        ).wait()

    for tick in range(WAVES + HOPS):
        if tick == 0:
            spread_wait(0)
            begin(0)
        if tick + 1 < WAVES:
            spread_wait(tick + 1)
            begin(tick + 1)
        for wave in range(WAVES):
            hop = tick - wave
            if 1 <= hop <= HOPS and not (wave == 4 and hop == 5):
                relay(wave, hop)
        done = tick - HOPS
        if tick == HOPS:
            for copy in consts:
                copy.wait()
        if 0 <= done < 4:
            transform(0, done, done, core * 64 + (done % 2) * 32 + 2 * plane + done // 2)
            if done % 2 == 1:
                transform(4, done - 1 + half, 4 + done // 2, 128 + core * 32 + 2 * plane + done // 2)
        if done == 3:
            for side in range(2):
                transform(4 * side, 4, 6 + side, 192 + core * 32 + side * 16 + plane)

    ring_finish()
    for slot in range(6):
        back_wait(slot)

    def basis_point(s, carry):
        lower = [halves(received[pl.ds(c * 16 + s, 128, stride=32), :]) for c in range(2)]
        upper = [halves(received[pl.ds(128 * 32 + c * 16 + s, 64, stride=32), :]) for c in range(2)]
        right = [
            jnp.concatenate(
                [
                    jnp.concatenate([lower[0][k], lower[1][k]], axis=1),
                    jnp.concatenate([-lower[1][k], lower[0][k]], axis=1),
                ],
                axis=0,
            )
            for k in range(2)
        ]
        left = [jnp.concatenate([upper[0][k], upper[1][k]], axis=1) for k in range(2)]
        both = dot(jnp.concatenate(left, axis=0), right[0])
        out = both[:64] + both[64:] + dot(left[0], right[1])
        for r in range(2):
            for c in range(2):
                products[rows(((r * 2 + c) * 16 + s) * 32, 32), :] = out[r * 32 : (r + 1) * 32, c * 128 : (c + 1) * 128]
        return carry

    lax.fori_loop(0, 16, basis_point, 0)

    def basis_copies(c):
        place = rows(c * 1024 + core * 512, 512)
        return (
            pltpu.make_async_copy(products.at[rows((core * 2 + c) * 512, 512)], basis_out.at[place], out_local.at[c]),
            pltpu.make_async_remote_copy(
                src_ref=products.at[rows(((1 - core) * 2 + c) * 512, 512)],
                dst_ref=basis_out.at[place],
                send_sem=out_send.at[c],
                recv_sem=out_recv.at[c],
                device_id=(half, point, 1 - core),
                device_id_type=MESH,
            ),
        )

    def residual_copies(c):
        place = rows(c * 32 + core * 16, 16)
        return (
            pltpu.make_async_copy(lanes.at[rows((core * 2 + c) * 16, 16)], residual_out.at[place], out_local.at[2 + c]),
            pltpu.make_async_remote_copy(
                src_ref=lanes.at[rows(((1 - core) * 2 + c) * 16, 16)],
                dst_ref=residual_out.at[place],
                send_sem=out_send.at[2 + c],
                recv_sem=out_recv.at[2 + c],
                device_id=(half, point, 1 - core),
                device_id_type=MESH,
            ),
        )

    for c in range(2):
        for copy in basis_copies(c):
            copy.start()

    for slot in range(6, 8):
        back_wait(slot)
    first_lane = lax.broadcasted_iota(jnp.int32, (64, 128), 1) < 64
    first_lane_s = lax.broadcasted_iota(jnp.int32, (16, 128), 1) < 64

    def residual_point(s, carry):
        left = []
        for c in range(2):
            left.append(
                jnp.concatenate(
                    [received[pl.ds((r * 64 + 32 * half) * 32 + c * 16 + s, 32, stride=32), :] for r in range(2)], axis=0
                )
            )
        left = halves(jnp.concatenate(left, axis=1))
        real = received[pl.ds(192 * 32 + s, 64, stride=32), :]
        imag = received[pl.ds(192 * 32 + 16 + s, 64, stride=32), :]
        real_turn = pltpu.roll(real, 64, 1)
        imag_turn = pltpu.roll(imag, 64, 1)
        mixed[pl.ds(0, 64, stride=2), :] = jnp.where(first_lane, real, imag_turn)
        mixed[pl.ds(1, 64, stride=2), :] = jnp.where(first_lane, real_turn, imag)
        mixed[pl.ds(128, 64, stride=2), :] = jnp.where(first_lane, -imag, real_turn)
        mixed[pl.ds(129, 64, stride=2), :] = jnp.where(first_lane, -imag_turn, real)
        right = halves(mixed[...])
        both = dot(jnp.concatenate(left, axis=0), right[0])
        pairs[rows(s * 64, 64), :] = both[:64] + both[64:] + dot(left[0], right[1])
        return carry

    lax.fori_loop(0, 16, residual_point, 0)

    for r in range(2):
        for k in range(16):
            even = pairs[pl.ds(r * 32 + 2 * k, 16, stride=64), :]
            odd = pairs[pl.ds(r * 32 + 2 * k + 1, 16, stride=64), :]
            lanes[pl.ds((r * 2) * 16, 16), k * 128 : (k + 1) * 128] = jnp.where(first_lane_s, even, pltpu.roll(odd, 64, 1))
            lanes[pl.ds((r * 2 + 1) * 16, 16), k * 128 : (k + 1) * 128] = jnp.where(first_lane_s, pltpu.roll(even, 64, 1), odd)

    for c in range(2):
        for copy in residual_copies(c):
            copy.start()
    for c in range(2):
        for copy in basis_copies(c) + residual_copies(c):
            copy.wait()


def per_device(children, residual_series):
    outer, inner = transform_matrices()
    vmem = pl.BlockSpec(memory_space=pltpu.VMEM)
    anywhere = pl.BlockSpec(memory_space=pl.ANY)
    basis, residual = pl.pallas_call(
        kernel,
        name="merge",
        out_shape=(
            jax.ShapeDtypeStruct((2 * WITHIN * 32, 128), F32),
            jax.ShapeDtypeStruct((2 * WITHIN, 2048), F32),
        ),
        in_specs=[vmem, vmem, anywhere, anywhere],
        out_specs=(anywhere, anywhere),
        scratch_shapes=[
            pltpu.VMEM((RING * WAVES * SLAB, 128), F32),
            pltpu.VMEM((WAVES * SLAB, 128), F32),
            pltpu.VMEM((2 * WITHIN * PLANE, 128), F32),
            pltpu.VMEM((8 * 1024, 128), F32),
            pltpu.VMEM((256 * 32, 128), F32),
            pltpu.VMEM((4 * 512, 128), F32),
            pltpu.VMEM((16 * 64, 128), F32),
            pltpu.VMEM((256, 128), F32),
            pltpu.VMEM((64, 2048), F32),
            pltpu.VMEM((32, 256), BF16),
            pltpu.VMEM((PLANE * 64, 256), BF16),
            pltpu.SemaphoreType.DMA((WAVES,)),
            pltpu.SemaphoreType.DMA((WAVES,)),
            pltpu.SemaphoreType.DMA((WAVES + 8,)),
            pltpu.SemaphoreType.DMA((WAVES * 2 * HOPS * PARTS,)),
            pltpu.SemaphoreType.DMA((WAVES * 2 * HOPS * PARTS,)),
            pltpu.SemaphoreType.DMA((8,)),
            pltpu.SemaphoreType.DMA((8,)),
            pltpu.SemaphoreType.DMA((2,)),
            pltpu.SemaphoreType.DMA((4,)),
            pltpu.SemaphoreType.DMA((4,)),
            pltpu.SemaphoreType.DMA((4,)),
        ],
        compiler_params=pltpu.CompilerParams(collective_id=0, has_side_effects=True, vmem_limit_bytes=48 * 2**20),
    )(
        children.reshape(WITHIN * 64, 128),
        residual_series,
        jnp.asarray(outer),
        jnp.asarray(inner),
    )
    return basis.reshape(2, WITHIN, 32, 128), residual.reshape(2, WITHIN, 2048)


def solution(mesh):
    placed = (P("half", "point", "row", None), P("point", ("row", "half")))
    return jax.shard_map(
        per_device,
        mesh=mesh,
        in_specs=placed,
        out_specs=(P(None, "point", ("row", "half"), None), P(None, "point", ("row", "half"))),
        check_vma=False,
    )
```

time: 523 us -> 157 us (0.30); the launches traced: 516 us -> 157 us
  waiting for transfers between devices: 187 us -> 0 us
  Pallas kernels: 0 us -> 150 us
  blocking collectives: 145 us -> 0 us
  local copies, waits for them, and re-layouts: 100 us -> 6.36 us
  matrix products: 51.3 us -> 0 us
  between operations: 14.4 us -> 0.65 us
  other arithmetic: 10.7 us -> 0 us
  starting transfers between devices: 7.59 us -> 0 us
    pallas_call x0 -> x1, Pallas kernels: none -> 150 us  [per_device(): pl.pallas_call(kernel, name='merge', out_shape=(jax.ShapeDtypeStruct((2 *...]
    all_to_all x1 -> x0, blocking collectives: 145 us -> none  [spectrum(): lax.all_to_all(evaluate(by_entry, groups, within), 'point', split_axis=1,...]
    all_gather x4 -> x0, waiting for transfers between devices: 115 us -> none  [the longest x1 70.9 us: per_device(): gathered = lax.all_gather(children, 'half', axis=0, tiled=True)]
    all_to_all x1 -> x0, waiting for transfers between devices: 71.3 us -> none  [spectrum(): lax.all_to_all(stacked, 'point', split_axis=1, concat_axis=0, tiled=True)]
    dot_general x14 -> x0, matrix products: 51.3 us -> none  [the longest x2 6.19 us: complex_product(): jnp.einsum('cik,ckj->cij', left_factor[0], right_factor[1], precision=hp)]
    another operation x5 -> x0, local copies, waits for them, and re-layouts: 48.9 us -> none  [the longest x2 47.3 us: evaluate(): jnp.stack([value_re.reshape(groups * within, entries), value_im.reshape(g...]
    all_to_all x4 -> x0, local copies, waits for them, and re-layouts: 20.1 us -> none  [the longest x2 13.2 us: spectrum(): lax.all_to_all(evaluate(by_entry, groups, within), 'point', split_axis=1,...]
    slice x4 -> x0, local copies, waits for them, and re-layouts: 10.8 us -> none  [the longest x1 4.64 us: per_device(): spectra[:, :, tile_size:2 * tile_size]]
  transfers between devices with their start and end apart: 5 -> 0, of which waited for: 5 -> 0; matrix products, arithmetic and copies ran while one was open for 6% -> 0% of each run, Pallas kernels for 0% -> 0%
where the time goes in v1:
time: 157 us
  Pallas kernels  150 us (96%)
  local copies, waits for them, and re-layouts  6.36 us (4%)
    pallas_call x1, Pallas kernels, per_device(): pl.pallas_call(kernel, name='merge', out_shape=(jax.ShapeDtypeStruct((2 *...  150 us
    unnamed x10, local copies, waits for them, and re-layouts  6.36 us

profile of v1, /device:TPU:1, one launch (start us, length us, event | category | flops | bytes accessed | tf_op | source)
XLA Modules:
  0.0 156.6 jit_solution(3275683949797221252)
XLA Ops:
  0.6 0.0 copy-start
  0.6 1.6 %copy-done = bf16[4,1024,256]{2,1,0:T(8,128)(2,1)S(1)} copy-done((bf16[4,1024,256]{2,1,0:T(8,128)(2,1)S(1)}, bf16[4,1024,256]{2,1,0:T(8,128)(2,1)}, u32[]{:S(2)}) %copy-start) | copy-done | bytes 2097176
  2.2 0.0 copy-start.1
  2.2 1.2 copy-done.1
  3.4 0.0 copy-start.2
  3.5 0.9 copy-done.2
  4.4 0.0 copy-start.3
  4.4 0.8 copy-done.3
  5.2 149.6 %merge.1 = (f32[2048,128]{1,0:T(8,128)S(1)}, f32[64,2048]{1,0:T(8,128)S(1)}) custom-call(f32[2048,128]{1,0:T(8,128)S(1)} %bitcast.3, f32[32,2048]{1,0:T(8,128)S(1)} %copy-done.2, bf16[4,32,256]{2,1,0:T(8,128)(2,1)S(1)} %copy-done.3, bf16[4,1024,256]{2,1,0:T(8,128)(2,1)S(1)} %copy-done), custom_call_target="tpu_custom_call" | custom-call | tf_op jit(solution)/shard_map/merge/pallas_call | solution.py:407
  154.9 1.0 copy.8
  155.8 0.8 copy.9
Async XLA Ops:
  0.6 1.6 %copy-start = (bf16[4,1024,256]{2,1,0:T(8,128)(2,1)S(1)}, bf16[4,1024,256]{2,1,0:T(8,128)(2,1)}, u32[]{:S(2)}) copy-start(bf16[4,1024,256]{2,1,0:T(8,128)(2,1)} %constant.5.clone.inner_all) | copy-start | bytes 6291460
  2.2 1.2 copy-start.1
  3.4 0.9 copy-start.2
  4.4 0.8 copy-start.3

commit v2 on v1

--- a/solution.py
+++ b/solution.py
@@ -20,6 +20,8 @@
 PARTS = 4
 SLAB = PLANE * WITHIN
 PART = SLAB // PARTS
+STARTS = {"L0": 1, "L1": 2, "L2": 3, "L3": 5, "U0": 1, "U1": 4, "S0": 8, "S1": 8}
+LEAD = 1
 MESH = pl.DeviceIdType.MESH
 F32 = jnp.float32
 BF16 = jnp.bfloat16
@@ -67,22 +69,42 @@
     return pl.ds(pl.multiple_of(offset, 8), count)
 
 
-def reach(wave, source, direction):
-    if wave == 4:
-        return 4 if direction == 0 else 3
-    lower = source + 2 if direction == 0 else 5 - source
-    if wave % 2 == 1:
-        upper = 7 - source if direction == 0 else source - 4
+def parts_of(item):
+    return range(2 * PARTS if item[0] == "U" else PARTS)
+
+
+def waves_of(item):
+    kind, number = item[0], int(item[1])
+    return {"L": [number], "U": [2 * number, 2 * number + 1], "S": [4]}[kind]
+
+
+def reach(item, source, direction, part):
+    in_lower = source < 4
+    if item[0] == "L":
+        return jnp.where(in_lower, source + 2 if direction == 0 else 5 - source, 0)
+    if item[0] == "S":
+        hops = 4 if (direction == 0) == (part < PARTS // 2) else 3
+        return jnp.where(in_lower if item == "S0" else source >= 4, hops, 0)
+    if part % 2 == 1:
+        hops = 7 - source if direction == 0 else source - 4
     elif direction == 0:
-        upper = jnp.where(source >= 6, 11 - source, 0)
+        hops = jnp.where(source >= 6, 11 - source, 0)
     else:
-        upper = jnp.where(source <= 5, source, 0)
-    return jnp.where(source < 4, lower, upper)
+        hops = jnp.where(source <= 5, source, 0)
+    return jnp.where(in_lower, 0, hops)
+
+
+def longest(item, direction, part):
+    if item[0] == "S":
+        return 4 if (direction == 0) == (part < PARTS // 2) else 3
+    if item[0] == "U" and part % 2 == 1:
+        return 3
+    return 5
 
 
 def kernel(
-    child, series, outer_all, inner_all, basis_out, residual_out,
-    gathered, sending, mid, spectra, received, products, pairs, mixed, lanes, outer, inner,
+    child_in, series_in, outer_all, inner_all, basis_out, residual_out,
+    child, series, gathered, sending, mid, spectra, received, products, pairs, mixed, lanes, outer, inner,
     a_send, a_recv, own_sem, z_send, z_recv, d_send, d_recv, const_sem, out_local, out_send, out_recv,
 ):
     half = lax.axis_index("half")
@@ -105,7 +127,11 @@
         pltpu.make_async_copy(outer_all.at[z], outer, const_sem.at[0]),
         pltpu.make_async_copy(inner_all.at[z], inner, const_sem.at[1]),
     ]
-    for copy in consts:
+    loads = [
+        pltpu.make_async_copy(child_in, child, const_sem.at[2]),
+        pltpu.make_async_copy(series_in, series, const_sem.at[3]),
+    ]
+    for copy in loads + consts:
         copy.start()
 
     barrier = pltpu.get_barrier_semaphore()
@@ -120,6 +146,8 @@
         pl.semaphore_signal(barrier, inc=1, device_id=ring_device((ring + step) % 8), device_id_type=MESH)
 
     for wave in range(WAVES):
+        if wave in (0, 4):
+            loads[wave // 4].wait()
         for m in range(PLANE):
             base = (wave * PLANE + m) * WITHIN
             if wave < 4:
@@ -132,10 +160,10 @@
     def slab(source, wave):
         return (source * WAVES + wave) * SLAB
 
-    for wave in range(WAVES):
+    def spread(wave):
         own = slab(ring, wave) + plane * WITHIN
 
-        def spread(i, carry):
+        def send(i, carry):
             peer = plane_peer(i)
             pltpu.make_async_remote_copy(
                 src_ref=sending.at[rows((wave * PLANE + peer) * WITHIN, WITHIN)],
@@ -147,7 +175,7 @@
             ).start()
             return carry
 
-        lax.fori_loop(1, PLANE, spread, 0)
+        lax.fori_loop(1, PLANE, send, 0)
         pltpu.make_async_copy(
             sending.at[rows((wave * PLANE + plane) * WITHIN, WITHIN)], gathered.at[rows(own, WITHIN)], own_sem.at[wave]
         ).start()
@@ -167,55 +195,64 @@
             sending.at[pl.ds(0, WITHIN)], gathered.at[rows(own, WITHIN)], own_sem.at[wave]
         ).wait()
 
-    def ring_copy(wave, direction, hop, part, source):
-        place = rows(slab(source, wave) + part * PART, PART)
-        target = ring_device((ring + (1 if direction == 0 else 7)) % 8)
-        index = ((wave * 2 + direction) * HOPS + hop) * PARTS + part
+    def ring_copy(item, direction, hop, part, source):
+        number = int(item[1])
+        if item[0] == "U":
+            offset = slab(source, 2 * number + part % 2) + part // 2 * PART
+            stream = 2 * number * PARTS + part
+        else:
+            wave = waves_of(item)[0]
+            offset = slab(source, wave) + part * PART
+            stream = wave * PARTS + part
+        place = rows(offset, PART)
+        index = (stream * 2 + direction) * HOPS + hop
         return pltpu.make_async_remote_copy(
             src_ref=gathered.at[place],
             dst_ref=gathered.at[place],
             send_sem=z_send.at[index],
             recv_sem=z_recv.at[index],
-            device_id=target,
+            device_id=ring_device((ring + (1 if direction == 0 else 7)) % 8),
             device_id_type=MESH,
         )
 
     def origin(direction, hop):
         return (ring + (8 - hop if direction == 0 else hop)) % 8
 
-    def begin(wave):
-        for part in range(PARTS):
+    def begin(item):
+        for part in parts_of(item):
             for direction in range(2):
 
-                @pl.when(reach(wave, ring, direction) >= 1)
+                @pl.when(reach(item, ring, direction, part) >= 1)
                 def _():
-                    ring_copy(wave, direction, 0, part, ring).start()
-
-    def relay(wave, hop):
-        for part in range(PARTS):
+                    ring_copy(item, direction, 0, part, ring).start()
+
+    def relay(item, hop):
+        for part in parts_of(item):
             for direction in range(2):
+                if longest(item, direction, part) < hop:
+                    continue
                 source = origin(direction, hop)
-                extent = reach(wave, source, direction)
+                extent = reach(item, source, direction, part)
 
                 @pl.when(extent >= hop)
                 def _():
-                    ring_copy(wave, direction, hop - 1, part, source).wait_recv()
-                    if hop < HOPS:
-
-                        @pl.when(extent >= hop + 1)
+                    ring_copy(item, direction, hop - 1, part, source).wait_recv()
+                    if longest(item, direction, part) > hop:
+
+                        @pl.when(extent > hop)
                         def _():
-                            ring_copy(wave, direction, hop, part, source).start()
+                            ring_copy(item, direction, hop, part, source).start()
 
     def ring_finish():
-        for wave in range(WAVES):
-            for hop in range(HOPS):
+        for item in STARTS:
+            for part in parts_of(item):
                 for direction in range(2):
-                    source = origin(direction, hop)
-
-                    @pl.when(reach(wave, source, direction) >= hop + 1)
-                    def _():
-                        for part in range(PARTS):
-                            ring_copy(wave, direction, hop, part, source).wait_send()
+                    for hop in range(longest(item, direction, part)):
+                        source = origin(direction, hop)
+
+                        @pl.when(reach(item, source, direction, part) > hop)
+                        def _():
+                            ring_copy(item, direction, hop, part, source).wait_send()
 
     def transform(first, wave, slot, place):
         def over_t(step, carry):
@@ -274,28 +311,38 @@
             spectra.at[pl.ds(0, 32)], received.at[pl.ds(0, 32)], own_sem.at[WAVES + slot]
         ).wait()
 
-    for tick in range(WAVES + HOPS):
-        if tick == 0:
-            spread_wait(0)
-            begin(0)
-        if tick + 1 < WAVES:
-            spread_wait(tick + 1)
-            begin(tick + 1)
-        for wave in range(WAVES):
-            hop = tick - wave
-            if 1 <= hop <= HOPS and not (wave == 4 and hop == 5):
-                relay(wave, hop)
-        done = tick - HOPS
-        if tick == HOPS:
-            for copy in consts:
-                copy.wait()
-        if 0 <= done < 4:
-            transform(0, done, done, core * 64 + (done % 2) * 32 + 2 * plane + done // 2)
-            if done % 2 == 1:
-                transform(4, done - 1 + half, 4 + done // 2, 128 + core * 32 + 2 * plane + done // 2)
-        if done == 3:
-            for side in range(2):
-                transform(4 * side, 4, 6 + side, 192 + core * 32 + side * 16 + plane)
+    for wave in range(WAVES):
+        spread(wave)
+
+    events = []
+    for item, start in STARTS.items():
+        last = 4 if item[0] == "S" else HOPS
+        events.append((start - LEAD, 1, start, item, 0))
+        events += [(start + hop, 0, start, item, hop) for hop in range(1, last + 1)]
+        events.append((start + last, 2, start, item, 0))
+    ready = set()
+    ready_consts = False
+    for _, kind, _, item, hop in sorted(events):
+        number = int(item[1])
+        if kind == 0:
+            relay(item, hop)
+        elif kind == 1:
+            for wave in waves_of(item):
+                if wave not in ready:
+                    spread_wait(wave)
+                    ready.add(wave)
+            begin(item)
+        else:
+            if not ready_consts:
+                for copy in consts:
+                    copy.wait()
+                ready_consts = True
+            if item[0] == "L":
+                transform(0, number, number, core * 64 + number % 2 * 32 + 2 * plane + number // 2)
+            elif item[0] == "U":
+                transform(4, 2 * number + half, 4 + number, 128 + core * 32 + 2 * plane + number)
+            else:
+                transform(4 * number, 4, 6 + number, 192 + core * 32 + number * 16 + plane)
 
     ring_finish()
     for slot in range(6):
@@ -402,8 +449,7 @@
 
 def per_device(children, residual_series):
     outer, inner = transform_matrices()
-    vmem = pl.BlockSpec(memory_space=pltpu.VMEM)
-    anywhere = pl.BlockSpec(memory_space=pl.ANY)
+    hbm = pl.BlockSpec(memory_space=pltpu.HBM)
     basis, residual = pl.pallas_call(
         kernel,
         name="merge",
@@ -411,9 +457,11 @@
             jax.ShapeDtypeStruct((2 * WITHIN * 32, 128), F32),
             jax.ShapeDtypeStruct((2 * WITHIN, 2048), F32),
         ),
-        in_specs=[vmem, vmem, anywhere, anywhere],
-        out_specs=(anywhere, anywhere),
+        in_specs=[hbm] * 4,
+        out_specs=(hbm, hbm),
         scratch_shapes=[
+            pltpu.VMEM((WITHIN * 64, 128), F32),
+            pltpu.VMEM((WITHIN, 2048), F32),
             pltpu.VMEM((RING * WAVES * SLAB, 128), F32),
             pltpu.VMEM((WAVES * SLAB, 128), F32),
             pltpu.VMEM((2 * WITHIN * PLANE, 128), F32),
@@ -428,16 +476,16 @@
             pltpu.SemaphoreType.DMA((WAVES,)),
             pltpu.SemaphoreType.DMA((WAVES,)),
             pltpu.SemaphoreType.DMA((WAVES + 8,)),
-            pltpu.SemaphoreType.DMA((WAVES * 2 * HOPS * PARTS,)),
-            pltpu.SemaphoreType.DMA((WAVES * 2 * HOPS * PARTS,)),
+            pltpu.SemaphoreType.DMA((WAVES * PARTS * 2 * HOPS,)),
+            pltpu.SemaphoreType.DMA((WAVES * PARTS * 2 * HOPS,)),
             pltpu.SemaphoreType.DMA((8,)),
             pltpu.SemaphoreType.DMA((8,)),
-            pltpu.SemaphoreType.DMA((2,)),
+            pltpu.SemaphoreType.DMA((4,)),
             pltpu.SemaphoreType.DMA((4,)),
             pltpu.SemaphoreType.DMA((4,)),
             pltpu.SemaphoreType.DMA((4,)),
         ],
-        compiler_params=pltpu.CompilerParams(collective_id=0, has_side_effects=True, vmem_limit_bytes=48 * 2**20),
+        compiler_params=pltpu.CompilerParams(collective_id=0, has_side_effects=True, vmem_limit_bytes=62 * 2**20),
     )(
         children.reshape(WITHIN * 64, 128),
         residual_series,

time: 157 us -> 146 us (0.930)
  Pallas kernels: 150 us -> 142 us
  local copies, waits for them, and re-layouts: 6.36 us -> 3.12 us
    pallas_call x1, Pallas kernels: 150 us -> 142 us  [per_device(): pl.pallas_call(kernel, name='merge', out_shape=(jax.ShapeDtypeStruct((2 *...]
    unnamed x10 -> x4, local copies, waits for them, and re-layouts: 6.36 us -> 3.12 us
where the time goes in v2:
time: 146 us; the launch traced here: 145 us
  Pallas kernels  142 us (97%)
  local copies, waits for them, and re-layouts  3.12 us (2%)
    pallas_call x1, Pallas kernels, per_device(): pl.pallas_call(kernel, name='merge', out_shape=(jax.ShapeDtypeStruct((2 *...  142 us
    unnamed x4, local copies, waits for them, and re-layouts  3.12 us

profile of v2, /device:TPU:1, one launch (start us, length us, event | category | flops | bytes accessed | tf_op | source)
XLA Modules:
  0.0 145.4 jit_solution(16413283037579687644)
XLA Ops:
  0.6 141.6 %merge.1 = (f32[2048,128]{1,0:T(8,128)}, f32[64,2048]{1,0:T(8,128)}) custom-call(f32[2048,128]{1,0:T(8,128)} %bitcast.3, f32[32,2048]{1,0:T(8,128)} %series_in.1, bf16[4,32,256]{2,1,0:T(8,128)(2,1)} %constant.4.clone.outer_all, bf16[4,1024,256]{2,1,0:T(8,128)(2,1)} %constant.5.clone.inner_all), custom_call_target="tpu_custom_call" | custom-call | tf_op jit(solution)/shard_map/merge/pallas_call | solution.py:453
  142.3 0.0 copy-start
  142.3 2.3 %copy.8 = f32[2,32,32,128]{3,2,1,0:T(8,128)} copy(f32[2,32,32,128]{3,2,1,0:T(8,128)} %bitcast.4) | data formatting | bytes 2097152
  144.6 0.0 copy-done
  144.6 0.8 copy.9
Async XLA Ops:
  142.3 2.3 %copy-start = (f32[64,2048]{1,0:T(8,128)S(1)}, f32[64,2048]{1,0:T(8,128)}, u32[]{:S(2)}) copy-start(f32[64,2048]{1,0:T(8,128)} %get-tuple-element.5) | copy-start | bytes 1572868

commit v3 on v2

--- a/solution.py
+++ b/solution.py
@@ -270,7 +270,7 @@
                 mid[rows((WITHIN + t) * PLANE, PLANE), :] = out[PLANE:, k * 128 : (k + 1) * 128]
             return carry
 
-        lax.fori_loop(0, WITHIN // 2, over_t, 0, unroll=2)
+        lax.fori_loop(0, WITHIN // 2, over_t, 0, unroll=16)
 
         def over_q(q, carry):
             values = mid[pl.ds(q, 2 * WITHIN, stride=PLANE), :]
@@ -278,7 +278,7 @@
             spectra[rows(slot * 1024 + q * 64, 64), :] = out
             return carry
 
-        lax.fori_loop(0, PLANE, over_q, 0, unroll=2)
+        lax.fori_loop(0, PLANE, over_q, 0, unroll=16)
 
         def back(i, carry):
             peer = plane_peer(i)
@@ -293,7 +293,7 @@
             ).start()
             return carry
 
-        lax.fori_loop(1, 32, back, 0)
+        lax.fori_loop(1, 32, back, 0, unroll=4)
         pltpu.make_async_copy(
             spectra.at[rows(slot * 1024 + plane * 64 + core * 32, 32)], received.at[rows(place * 32, 32)], own_sem.at[WAVES + slot]
         ).start()
@@ -369,7 +369,7 @@
                 products[rows(((r * 2 + c) * 16 + s) * 32, 32), :] = out[r * 32 : (r + 1) * 32, c * 128 : (c + 1) * 128]
         return carry
 
-    lax.fori_loop(0, 16, basis_point, 0)
+    lax.fori_loop(0, 16, basis_point, 0, unroll=2)
 
     def basis_copies(c):
         place = rows(c * 1024 + core * 512, 512)
@@ -430,7 +430,7 @@
         pairs[rows(s * 64, 64), :] = both[:64] + both[64:] + dot(left[0], right[1])
         return carry
 
-    lax.fori_loop(0, 16, residual_point, 0)
+    lax.fori_loop(0, 16, residual_point, 0, unroll=2)
 
     for r in range(2):
         for k in range(16):

time: 146 us -> 141 us (0.966)
  Pallas kernels: 142 us -> 137 us
    pallas_call x1, Pallas kernels: 142 us -> 137 us  [per_device(): pl.pallas_call(kernel, name='merge', out_shape=(jax.ShapeDtypeStruct((2 *...]
where the time goes in v3:
time: 141 us; the launch traced here: 140 us
  Pallas kernels  137 us (97%)
  local copies, waits for them, and re-layouts  3.12 us (2%)
    pallas_call x1, Pallas kernels, per_device(): pl.pallas_call(kernel, name='merge', out_shape=(jax.ShapeDtypeStruct((2 *...  137 us
    unnamed x4, local copies, waits for them, and re-layouts  3.12 us

profile of v3, /device:TPU:1, one launch (start us, length us, event | category | flops | bytes accessed | tf_op | source)
XLA Modules:
  0.0 140.4 jit_solution(10096217498982775655)
XLA Ops:
  0.6 136.6 %merge.1 = (f32[2048,128]{1,0:T(8,128)}, f32[64,2048]{1,0:T(8,128)}) custom-call(f32[2048,128]{1,0:T(8,128)} %bitcast.3, f32[32,2048]{1,0:T(8,128)} %series_in.1, bf16[4,32,256]{2,1,0:T(8,128)(2,1)} %constant.4.clone.outer_all, bf16[4,1024,256]{2,1,0:T(8,128)(2,1)} %constant.5.clone.inner_all), custom_call_target="tpu_custom_call" | custom-call | tf_op jit(solution)/shard_map/merge/pallas_call | solution.py:453
  137.3 0.0 copy-start
  137.3 2.3 %copy.8 = f32[2,32,32,128]{3,2,1,0:T(8,128)} copy(f32[2,32,32,128]{3,2,1,0:T(8,128)} %bitcast.4) | data formatting | bytes 2097152
  139.6 0.0 copy-done
  139.6 0.8 copy.9
Async XLA Ops:
  137.3 2.3 %copy-start = (f32[64,2048]{1,0:T(8,128)S(1)}, f32[64,2048]{1,0:T(8,128)}, u32[]{:S(2)}) copy-start(f32[64,2048]{1,0:T(8,128)} %get-tuple-element.5) | copy-start | bytes 1572868

commit v4 on v3

--- a/solution.py
+++ b/solution.py
@@ -17,11 +17,11 @@
 RING = 8
 WAVES = 5
 HOPS = 5
-PARTS = 4
+PARTS = 2
 SLAB = PLANE * WITHIN
 PART = SLAB // PARTS
-STARTS = {"L0": 1, "L1": 2, "L2": 3, "L3": 5, "U0": 1, "U1": 4, "S0": 8, "S1": 8}
-LEAD = 1
+STARTS = {'L0': 0, 'L1': 1, 'L2': 5, 'L3': 3, 'U0': 0, 'U1': 3, 'S0': 8, 'S1': 8}
+LEAD = 0
 MESH = pl.DeviceIdType.MESH
 F32 = jnp.float32
 BF16 = jnp.bfloat16

time: 141 us -> 140 us (level)
  no operation moved by 1% of the time
where the time goes in v4:
time: 140 us
  Pallas kernels  136 us (97%)
  local copies, waits for them, and re-layouts  3.12 us (2%)
    pallas_call x1, Pallas kernels, per_device(): pl.pallas_call(kernel, name='merge', out_shape=(jax.ShapeDtypeStruct((2 *...  136 us
    unnamed x4, local copies, waits for them, and re-layouts  3.12 us

profile of v4, /device:TPU:1, one launch (start us, length us, event | category | flops | bytes accessed | tf_op | source)
XLA Modules:
  0.0 139.6 jit_solution(9174402489373920862)
XLA Ops:
  0.6 135.8 %merge.1 = (f32[2048,128]{1,0:T(8,128)}, f32[64,2048]{1,0:T(8,128)}) custom-call(f32[2048,128]{1,0:T(8,128)} %bitcast.3, f32[32,2048]{1,0:T(8,128)} %series_in.1, bf16[4,32,256]{2,1,0:T(8,128)(2,1)} %constant.4.clone.outer_all, bf16[4,1024,256]{2,1,0:T(8,128)(2,1)} %constant.5.clone.inner_all), custom_call_target="tpu_custom_call" | custom-call | tf_op jit(solution)/shard_map/merge/pallas_call | solution.py:453
  136.5 0.0 copy-start
  136.5 2.3 %copy.8 = f32[2,32,32,128]{3,2,1,0:T(8,128)} copy(f32[2,32,32,128]{3,2,1,0:T(8,128)} %bitcast.4) | data formatting | bytes 2097152
  138.8 0.0 copy-done
  138.8 0.8 copy.9
Async XLA Ops:
  136.5 2.3 %copy-start = (f32[64,2048]{1,0:T(8,128)S(1)}, f32[64,2048]{1,0:T(8,128)}, u32[]{:S(2)}) copy-start(f32[64,2048]{1,0:T(8,128)} %get-tuple-element.5) | copy-start | bytes 1572868
